TPU v7x, 256 devices: a whole 4x4x8 slice. The times are simulated.
256 devices in a mesh: dp: 4 (over y), row: 4 (over z_lo, core), col: 16 (over x, z_hi).
Axes of the slice: x: 4, y: 4, z: 8 (z_hi: 4, z_lo: 2; z = z_hi * 2 + z_lo), core: 2. Of those that a mesh axis runs over, the one named last changes fastest.
Arguments:
- tokens: bfloat16 [4096, 12288], P(('dp', 'col'), 'row'), may hold values from -6 to 6
- w_tiles: bfloat16 [4, 192, 8, 128, 128], P('row', 'col'), may hold values from -0.1875 to 0.1875
- tile_rows: int32 [4, 192, 8], P('row', 'col'), may hold values from 0 to 23, as said below
- tile_count: int32 [4, 192], P('row', 'col'), may hold values from 2 to 8, as said below
- grad_hidden: bfloat16 [4096, 24576], P(('dp', 'row'), 'col'), may hold values from -6 to 6
Outputs:
- hidden: bfloat16 [4096, 24576], P(('dp', 'row'), 'col')
- grad_tokens: bfloat16 [4096, 12288], P(('dp', 'col'), 'row')
- grad_weights: bfloat16 [4, 192, 8, 128, 128], P('row', 'col')
Inputs may be any that keep to these rules, and one draw needn't show every extreme that they name: `tile_rows`: within each row group and panel the 8 entries are distinct. `tile_count`: in every row group some panel has exactly 8 live slots.
All inputs are finite; a program needn't handle non-finite values.
Results may differ from a plain program's by a relative error of at most 0.02.
Values may be sent and summed in bfloat16 or wider, within the bound.
No kernel may reach another device: no remote copies, remote signals or barrier semaphores. Data moves between devices by JAX's collectives and lax.ppermute only.
A program may use at most 128 MiB of HBM per device.

v0:
```python
from functools import partial
import math

import jax
import jax.numpy as jnp
from jax import lax
from jax.sharding import PartitionSpec as P


def settle(values):
    return lax.optimization_barrier(values.astype(jnp.bfloat16)).astype(jnp.float32)


def local(tokens, w_tiles, tile_rows, tile_count, grad_hidden):
    tile_size = w_tiles.shape[-1]
    slot_count = w_tiles.shape[2]
    panels = w_tiles.shape[1]
    feat_width = tokens.shape[1]
    group_blocks = feat_width // tile_size
    slot_rows = tile_rows[0]
    flat_rows = slot_rows.reshape(panels * slot_count)
    live_slot = jnp.arange(slot_count)[None, :] < tile_count[0][:, None]
    masked = w_tiles[0] * live_slot[:, :, None, None].astype(jnp.bfloat16)

    def select(row_block):
        shaped = row_block.reshape(row_block.shape[0], group_blocks, tile_size)
        return jnp.take(shaped, slot_rows, axis=1)

    gathered = lax.all_gather(tokens, "col", axis=0, tiled=True)
    all_count = gathered.shape[0]
    row_count = lax.axis_size("row") * grad_hidden.shape[0]
    block_rows = math.gcd(row_count, 256)
    blocks_in = gathered
    blocks_in = blocks_in.reshape(row_count // block_rows, block_rows, feat_width)

    def hidden_per_block(row_block):
        spread = jnp.einsum(
            "tpkb,pkbc->tpc", select(row_block), masked, preferred_element_type=jnp.float32
        )
        return settle(spread.reshape(block_rows, panels * tile_size))

    pre_act = lax.psum_scatter(
        lax.map(hidden_per_block, blocks_in)
        .reshape(row_count, panels * tile_size)
        .astype(jnp.bfloat16),
        "row",
        scatter_dimension=0,
        tiled=True,
    ).astype(jnp.float32)
    gelu_fn = partial(jax.nn.gelu, approximate=True)
    hidden = gelu_fn(pre_act).astype(jnp.bfloat16)
    _, backward = jax.vjp(gelu_fn, pre_act)
    grad_pre = backward(grad_hidden.astype(jnp.float32))[0].astype(jnp.bfloat16)
    grad_all = lax.all_gather(grad_pre, "row", axis=0, tiled=True)
    row_count = lax.axis_size("col") * tokens.shape[0]
    input_block_rows = math.gcd(row_count, 128)
    blocks_in = grad_all
    blocks_in = blocks_in.reshape(
        row_count // input_block_rows, input_block_rows, panels, tile_size
    )

    def input_per_block(row_block):
        spread = jnp.einsum("tpc,pkbc->tpkb", row_block, masked, preferred_element_type=jnp.float32)
        spread = spread.reshape(input_block_rows, panels * slot_count, tile_size)
        placed = jnp.zeros((input_block_rows, group_blocks, tile_size), jnp.float32)
        placed = placed.at[:, flat_rows, :].add(spread)
        return settle(placed.reshape(input_block_rows, feat_width))

    grad_tokens = lax.psum_scatter(
        lax.map(input_per_block, blocks_in).reshape(row_count, feat_width).astype(jnp.bfloat16),
        "col",
        scatter_dimension=0,
        tiled=True,
    )
    weight_block_rows = math.gcd(all_count, 256)
    source_blocks = gathered.reshape(all_count // weight_block_rows, weight_block_rows, feat_width)
    grad_blocks = grad_all.reshape(
        all_count // weight_block_rows, weight_block_rows, panels, tile_size
    )

    def accumulate(carry, block_pair):
        row_block, grad_block = block_pair
        update = jnp.einsum(
            "tpkb,tpc->pkbc", select(row_block), grad_block, preferred_element_type=jnp.float32
        )
        return (carry + update, None)

    start_grad = jnp.zeros((panels, slot_count, tile_size, tile_size), jnp.float32)
    local_grad, _ = lax.scan(accumulate, start_grad, (source_blocks, grad_blocks))
    local_grad = settle(local_grad * live_slot[:, :, None, None].astype(jnp.float32))
    summed = lax.psum(local_grad.astype(jnp.bfloat16), "dp")
    return (hidden, grad_tokens, summed[None])


def solution(mesh):
    placed = (
        P(("dp", "col"), "row"),
        P("row", "col", None, None, None),
        P("row", "col", None),
        P("row", "col"),
        P(("dp", "row"), "col"),
    )
    return jax.shard_map(
        local,
        mesh=mesh,
        in_specs=placed,
        out_specs=(
            P(("dp", "row"), "col"),
            P(("dp", "col"), "row"),
            P("row", "col", None, None, None),
        ),
        check_vma=False,
    )
```

profile of v0, /device:TPU:8, one launch (start us, length us, event | category | flops | bytes accessed | tf_op | source)
XLA Modules:
  0.0 719.6 jit_solution(5412630340526150167)
XLA Ops:
  14.9 95.6 %all-gather.3.cloned.1.call-done = bf16[1024,3072]{1,0:T(8,128)(2,1)} async-done(((bf16[64,3072]{1,0:T(8,128)(2,1)}), bf16[1024,3072]{1,0:T(8,128)(2,1)}) %all-gather.3.cloned.1.call-update) | async-done | bytes 6291472 | tf_op jit(solution)/shard_map/all_gather | solution.py:29
  110.5 8.7 %copy.45 = bf16[4,256,3072]{1,2,0:T(8,128)(2,1)} copy(bf16[4,256,3072]{2,1,0:T(8,128)(2,1)} %bitcast.104) | data formatting | bytes 12582912 | tf_op jit(solution)/shard_map/while | solution.py:43
  119.2 65.6 %while.31 = (s32[]{:T(128)}, bf16[4,256,1536]{1,2,0:T(8,128)(2,1)}, bf16[4,256,3072]{1,2,0:T(8,128)(2,1)}, s32[12,8]{1,0:T(8,128)S(1)}, bf16[12,8,128,128]{2,3,1,0:T(8,128)(2,1)}, /*index=5*/s32[]{:T(128)}) while((s32[]{:T(128)}, bf16[4,256,1536]{1,2,0:T(8,128)(2,1)}, bf16[4,256,3072]{1,2,0:T(8,128)(2,1)}, s32[12,8]{1,0:T(8,128)S(1)}, ...), condition=%wide.region_1.0_spmd, body=%wide.region_0.2_spmd.sunk | while | flops 809240448 | bytes 56630220 | solution.py:43
  127.7 6.1 bitcast_convert_fusion.2
  144.1 6.1 bitcast_convert_fusion.2
  160.5 6.1 bitcast_convert_fusion.2
  176.9 6.1 bitcast_convert_fusion.2
  189.6 38.0 %reduce-scatter.3.cloned.1.call-done = bf16[256,1536]{1,0:T(8,128)(2,1)} async-done(((bf16[1024,1536]{1,0:T(8,128)(2,1)}), bf16[256,1536]{1,0:T(8,128)(2,1)}) %reduce-scatter.3.cloned.1.call-update) | async-done | bytes 786448 | tf_op jit(solution)/shard_map/reduce_scatter | solution.py:42
  231.5 40.2 %all-gather.5.cloned.1.call-done = bf16[1024,1536]{1,0:T(8,128)(2,1)} async-done(((bf16[256,1536]{1,0:T(8,128)(2,1)}), bf16[1024,1536]{1,0:T(8,128)(2,1)}) %all-gather.5.cloned.1.call-update) | async-done | bytes 3145744 | tf_op jit(solution)/shard_map/all_gather | solution.py:54
  271.7 6.9 reshape.149
  291.9 104.6 %while.33 = (s32[]{:T(128)}, f32[12,8,128,128]{3,2,1,0:T(8,128)}, bf16[4,256,3072]{1,2,0:T(8,128)(2,1)}, s32[12,8]{1,0:T(8,128)S(1)}, bf16[4,256,12,128]{3,1,2,0:T(8,128)(2,1)}, /*index=5*/s32[]{:T(128)}, s32[]{:T(128)}) while((s32[]{:T(128)}, f32[12,8,128,128]{3,2,1,0:T(8,128)}, bf16[4,256,3072]{1,2,0:T(8,128)(2,1)}, ...), condition=%wide.region_8.10_spmd.clone, body=%wide.region_7.9_spmd.clone.sunk | while | flops 811599744 | bytes 51125156 | solution.py:89
  294.4 6.1 gather_fusion.1
  300.5 8.7 %copy.71 = bf16[12,8,256,128]{2,3,1,0:T(8,128)(2,1)} copy(bf16[12,8,256,128]{3,2,1,0:T(8,128)(2,1)} %bitcast.95) | data formatting | bytes 12582912 | tf_op jit(solution)/shard_map/while/body/eval_jaxpr/jit(_take)/gather | solution.py:27
  309.2 7.4 %select_add_fusion.2 = f32[12,8,128,128]{3,2,1,0:T(8,128)} fusion(f32[12,8,128,128]{3,2,1,0:T(8,128)} %get-tuple-element.340, pred[]{:T(512)S(6)} %compare.3, bf16[12,8,256,128]{2,3,1,0:T(8,128)(2,1)} %copy.71, pred[12,8]{1,0:T(8,128)(4,1)S(1)} %compare_and_fusion.5, bf16[4,256,12,128]{3,1,2,0:T(8,128)(2,1)} %get-tuple-element.350, s32[]{:T(128)S(6)} %copy.89), kind=kOutput, calls=%fused_computation.25.clone.1 | convolution fusion | flops 811597824 | bytes 19660900 | tf_op jit(solution)/shard_map/while/body/eval_jaxpr/tpkb,tpc->pkbc/dot_general | solution.py:83
  325.2 8.7 %copy.71 = bf16[12,8,256,128]{2,3,1,0:T(8,128)(2,1)} copy(bf16[12,8,256,128]{3,2,1,0:T(8,128)(2,1)} %bitcast.95) | data formatting | bytes 12582912 | tf_op jit(solution)/shard_map/while/body/eval_jaxpr/jit(_take)/gather | solution.py:27
  334.0 9.3 %select_add_fusion.2 = f32[12,8,128,128]{3,2,1,0:T(8,128)} fusion(f32[12,8,128,128]{3,2,1,0:T(8,128)} %get-tuple-element.340, pred[]{:T(512)S(6)} %compare.3, bf16[12,8,256,128]{2,3,1,0:T(8,128)(2,1)} %copy.71, pred[12,8]{1,0:T(8,128)(4,1)S(1)} %compare_and_fusion.5, bf16[4,256,12,128]{3,1,2,0:T(8,128)(2,1)} %get-tuple-element.350, s32[]{:T(128)S(6)} %copy.89), kind=kOutput, calls=%fused_computation.25.clone.1 | convolution fusion | flops 811597824 | bytes 19660900 | tf_op jit(solution)/shard_map/while/body/eval_jaxpr/tpkb,tpc->pkbc/dot_general | solution.py:83
  345.8 6.1 gather_fusion.1
  351.8 8.7 %copy.71 = bf16[12,8,256,128]{2,3,1,0:T(8,128)(2,1)} copy(bf16[12,8,256,128]{3,2,1,0:T(8,128)(2,1)} %bitcast.95) | data formatting | bytes 12582912 | tf_op jit(solution)/shard_map/while/body/eval_jaxpr/jit(_take)/gather | solution.py:27
  360.6 9.3 %select_add_fusion.2 = f32[12,8,128,128]{3,2,1,0:T(8,128)} fusion(f32[12,8,128,128]{3,2,1,0:T(8,128)} %get-tuple-element.340, pred[]{:T(512)S(6)} %compare.3, bf16[12,8,256,128]{2,3,1,0:T(8,128)(2,1)} %copy.71, pred[12,8]{1,0:T(8,128)(4,1)S(1)} %compare_and_fusion.5, bf16[4,256,12,128]{3,1,2,0:T(8,128)(2,1)} %get-tuple-element.350, s32[]{:T(128)S(6)} %copy.89), kind=kOutput, calls=%fused_computation.25.clone.1 | convolution fusion | flops 811597824 | bytes 19660900 | tf_op jit(solution)/shard_map/while/body/eval_jaxpr/tpkb,tpc->pkbc/dot_general | solution.py:83
  378.5 8.7 %copy.71 = bf16[12,8,256,128]{2,3,1,0:T(8,128)(2,1)} copy(bf16[12,8,256,128]{3,2,1,0:T(8,128)(2,1)} %bitcast.95) | data formatting | bytes 12582912 | tf_op jit(solution)/shard_map/while/body/eval_jaxpr/jit(_take)/gather | solution.py:27
  387.2 9.3 %select_add_fusion.2 = f32[12,8,128,128]{3,2,1,0:T(8,128)} fusion(f32[12,8,128,128]{3,2,1,0:T(8,128)} %get-tuple-element.340, pred[]{:T(512)S(6)} %compare.3, bf16[12,8,256,128]{2,3,1,0:T(8,128)(2,1)} %copy.71, pred[12,8]{1,0:T(8,128)(4,1)S(1)} %compare_and_fusion.5, bf16[4,256,12,128]{3,1,2,0:T(8,128)(2,1)} %get-tuple-element.350, s32[]{:T(128)S(6)} %copy.89), kind=kOutput, calls=%fused_computation.25.clone.1 | convolution fusion | flops 811597824 | bytes 19660900 | tf_op jit(solution)/shard_map/while/body/eval_jaxpr/tpkb,tpc->pkbc/dot_general | solution.py:83
  403.4 187.2 %while.32 = (s32[]{:T(128)}, bf16[8,128,3072]{1,2,0:T(8,128)(2,1)}, s32[96]{0:T(128)S(1)}, bf16[8,128,12,128]{3,1,2,0:T(8,128)(2,1)}, bf16[12,8,128,128]{3,2,1,0...) while((s32[]{:T(128)}, bf16[8,128,3072]{1,2,0:T(8,128)(2,1)}, ...), condition=%wide.region_5.7_spmd, body=%wide.region_3.6_spmd.sunk | while | flops 405012768 | bytes 49153284 | solution.py:70
  408.2 13.1 %scatter_fusion = f32[128,24,128]{2,0,1:T(8,128)S(1)} fusion(f32[128,24,128]{2,0,1:T(8,128)S(1)} %broadcast.145, s32[96]{0:T(128)S(1)} %fusion.51, f32[96,128,128]{2,1,0:T(8,128)} %bitcast.94), kind=kCustom, calls=%fused_computation.2.clone.1 | custom fusion | flops 1572864 | bytes 18874752 | tf_op jit(solution)/shard_map/while/body/eval_jaxpr/scatter-add | solution.py:66
  431.8 13.1 %scatter_fusion = f32[128,24,128]{2,0,1:T(8,128)S(1)} fusion(f32[128,24,128]{2,0,1:T(8,128)S(1)} %broadcast.145, s32[96]{0:T(128)S(1)} %fusion.51, f32[96,128,128]{2,1,0:T(8,128)} %bitcast.94), kind=kCustom, calls=%fused_computation.2.clone.1 | custom fusion | flops 1572864 | bytes 18874752 | tf_op jit(solution)/shard_map/while/body/eval_jaxpr/scatter-add | solution.py:66
  455.2 13.0 %scatter_fusion = f32[128,24,128]{2,0,1:T(8,128)S(1)} fusion(f32[128,24,128]{2,0,1:T(8,128)S(1)} %broadcast.145, s32[96]{0:T(128)S(1)} %fusion.51, f32[96,128,128]{2,1,0:T(8,128)} %bitcast.94), kind=kCustom, calls=%fused_computation.2.clone.1 | custom fusion | flops 1572864 | bytes 18874752 | tf_op jit(solution)/shard_map/while/body/eval_jaxpr/scatter-add | solution.py:66
  478.7 12.9 %scatter_fusion = f32[128,24,128]{2,0,1:T(8,128)S(1)} fusion(f32[128,24,128]{2,0,1:T(8,128)S(1)} %broadcast.145, s32[96]{0:T(128)S(1)} %fusion.51, f32[96,128,128]{2,1,0:T(8,128)} %bitcast.94), kind=kCustom, calls=%fused_computation.2.clone.1 | custom fusion | flops 1572864 | bytes 18874752 | tf_op jit(solution)/shard_map/while/body/eval_jaxpr/scatter-add | solution.py:66
  502.1 12.9 %scatter_fusion = f32[128,24,128]{2,0,1:T(8,128)S(1)} fusion(f32[128,24,128]{2,0,1:T(8,128)S(1)} %broadcast.145, s32[96]{0:T(128)S(1)} %fusion.51, f32[96,128,128]{2,1,0:T(8,128)} %bitcast.94), kind=kCustom, calls=%fused_computation.2.clone.1 | custom fusion | flops 1572864 | bytes 18874752 | tf_op jit(solution)/shard_map/while/body/eval_jaxpr/scatter-add | solution.py:66
  525.5 12.9 %scatter_fusion = f32[128,24,128]{2,0,1:T(8,128)S(1)} fusion(f32[128,24,128]{2,0,1:T(8,128)S(1)} %broadcast.145, s32[96]{0:T(128)S(1)} %fusion.51, f32[96,128,128]{2,1,0:T(8,128)} %bitcast.94), kind=kCustom, calls=%fused_computation.2.clone.1 | custom fusion | flops 1572864 | bytes 18874752 | tf_op jit(solution)/shard_map/while/body/eval_jaxpr/scatter-add | solution.py:66
  548.8 12.9 %scatter_fusion = f32[128,24,128]{2,0,1:T(8,128)S(1)} fusion(f32[128,24,128]{2,0,1:T(8,128)S(1)} %broadcast.145, s32[96]{0:T(128)S(1)} %fusion.51, f32[96,128,128]{2,1,0:T(8,128)} %bitcast.94), kind=kCustom, calls=%fused_computation.2.clone.1 | custom fusion | flops 1572864 | bytes 18874752 | tf_op jit(solution)/shard_map/while/body/eval_jaxpr/scatter-add | solution.py:66
  572.1 12.9 %scatter_fusion = f32[128,24,128]{2,0,1:T(8,128)S(1)} fusion(f32[128,24,128]{2,0,1:T(8,128)S(1)} %broadcast.145, s32[96]{0:T(128)S(1)} %fusion.51, f32[96,128,128]{2,1,0:T(8,128)} %bitcast.94), kind=kCustom, calls=%fused_computation.2.clone.1 | custom fusion | flops 1572864 | bytes 18874752 | tf_op jit(solution)/shard_map/while/body/eval_jaxpr/scatter-add | solution.py:66
  590.6 8.7 %copy.52 = bf16[8,128,3072]{2,1,0:T(8,128)(2,1)} copy(bf16[8,128,3072]{1,2,0:T(8,128)(2,1)} %get-tuple-element.362) | data formatting | bytes 12582912 | tf_op jit(solution)/shard_map/convert_element_type | solution.py:70
  599.3 109.8 %reduce-scatter.5.cloned.1.call-done = bf16[64,3072]{1,0:T(8,128)(2,1)} async-done(((bf16[1024,3072]{1,0:T(8,128)(2,1)}), bf16[64,3072]{1,0:T(8,128)(2,1)}) %reduce-scatter.5.cloned.1.call-update) | async-done | bytes 393232 | tf_op jit(solution)/shard_map/reduce_scatter | solution.py:69
  (175 shorter events, 186.9 us)
Async XLA Ops:
  7.2 103.4 %all-gather.3.cloned.1.call-start = ((), (), s32[]{:S(2)}) async-start(), calls=%async_computation.2 | async-start | bytes 6684672 | tf_op jit(solution)/shard_map/all_gather | solution.py:29
  7.9 219.6 %reduce-scatter.3.cloned.1.call-start = ((), (), s32[]{:S(2)}) async-start(), calls=%async_computation.3 | async-start | bytes 3932160 | tf_op jit(solution)/shard_map/reduce_scatter | solution.py:42
  11.6 3.3 copy-start
  127.7 6.1 copy-start.4
  133.9 1.7 copy-start.5
  144.1 6.1 copy-start.4
  150.3 1.7 copy-start.5
  160.5 6.1 copy-start.4
  166.7 1.7 copy-start.5
  176.9 6.1 copy-start.4
  183.1 1.7 copy-start.5
  189.5 38.0 %copy-start.6 = (bf16[256,1536]{1,0:T(8,128)(2,1)S(1)}, bf16[256,1536]{1,0:T(8,128)(2,1)}, u32[]{:S(2)}) copy-start(bf16[256,1536]{1,0:T(8,128)(2,1)} %param.17) | copy-start | bytes 2359300
  189.5 41.8 %copy-start.7 = (s32[1,12,8]{1,2,0:T(8,128)S(1)}, s32[1,12,8]{1,2,0:T(8,128)}, u32[]{:S(2)}) copy-start(s32[1,12,8]{1,2,0:T(8,128)} %param.15) | copy-start | bytes 1156
  189.5 82.2 %all-gather.5.cloned.1.call-start = ((), (), s32[]{:S(2)}) async-start(), calls=%async_computation.4 | async-start | bytes 3932160 | tf_op jit(solution)/shard_map/all_gather | solution.py:54
  231.1 368.2 %all-reduce.2.cloned.1.call-start = ((), (), s32[]{:S(2)}) async-start(), calls=%async_computation.6 | async-start | bytes 6291456 | tf_op jit(solution)/shard_map/psum | solution.py:91
  278.6 4.9 copy-start.3
  401.5 1.9 copy-start.1
  401.5 307.6 %reduce-scatter.5.cloned.1.call-start = ((), (), s32[]{:S(2)}) async-start(), calls=%async_computation.5 | async-start | bytes 6684672 | tf_op jit(solution)/shard_map/reduce_scatter | solution.py:69
  422.4 4.6 copy-start.2
  445.9 4.5 copy-start.2
  469.3 4.6 copy-start.2
  492.7 4.6 copy-start.2
  516.1 4.5 copy-start.2
  539.4 4.5 copy-start.2
  562.7 4.5 copy-start.2
  586.0 4.5 copy-start.2
Sparse Core Ops, SparseCore 0:
  10.5 100.0 all-gather.2
  189.6 37.8 reduce-scatter.2
  231.2 40.4 all-gather.4
  401.7 80.3 all-reduce.1
  599.4 109.6 reduce-scatter.4
where the time goes:
time: 724 us; the launch traced here: 720 us
  waiting for transfers between devices  284 us (39%)
  local copies, waits for them, and re-layouts  183 us (25%)
  other arithmetic  141 us (19%)
  matrix products  96.8 us (13%)
  between operations  13.8 us (2%)
    reduce_scatter x1, waiting for transfers between devices, local(): lax.psum_scatter(lax.map(input_per_block, blocks_in).reshape(row_count, f...  110 us
    scatter-add x8, other arithmetic, input_per_block(): placed = placed.at[:, flat_rows, :].add(spread)  104 us
    all_gather x1, waiting for transfers between devices, local(): gathered = lax.all_gather(tokens, 'col', axis=0, tiled=True)  95.6 us
    gather x12, local copies, waits for them, and re-layouts, select(): return jnp.take(shaped, slot_rows, axis=1)  83.2 us
    all_gather x1, waiting for transfers between devices, local(): grad_all = lax.all_gather(grad_pre, 'row', axis=0, tiled=True)  40.2 us
    reduce_scatter x1, waiting for transfers between devices, local(): lax.psum_scatter(lax.map(hidden_per_block, blocks_in).reshape(row_count,...  38 us
    dot_general x8, matrix products, input_per_block(): jnp.einsum('tpc,pkbc->tpkb', row_block, masked, preferred_element_type=jn...  37.1 us
    dot_general x4, matrix products, accumulate(): jnp.einsum('tpkb,tpc->pkbc', select(row_block), grad_block, preferred_ele...  35.2 us
  transfers between devices with their start and end apart: 5, of which 4 were waited for; matrix products, arithmetic and copies ran while one was open for 28% of the time, Pallas kernels for 0%

commit v1 on v0

v1 whole, which is shorter than its diff:
```python
from functools import partial

import jax
import jax.numpy as jnp
from jax import lax
from jax.experimental import pallas as pl
from jax.experimental.pallas import tpu as pltpu
from jax.sharding import PartitionSpec as P

VMEM_LIMIT = 48 * 1024 * 1024


def lanes(start, size):
    return pl.ds(pl.multiple_of(start * size, size), size)


def forward_kernel(rows, count, x_ref, w_ref, o_ref):
    panel = pl.program_id(0)
    slots, tile, _ = w_ref.shape[1:]
    live = count[panel]
    weights = jnp.concatenate(
        [w_ref[0, k] * (live > k).astype(jnp.bfloat16) for k in range(slots)], axis=0
    )
    block = 256

    def body(i, carry):
        at = pl.ds(pl.multiple_of(i * block, block), block)
        chosen = [x_ref[at, lanes(rows[panel * slots + k], tile)] for k in range(slots)]
        total = jnp.dot(
            jnp.concatenate(chosen, axis=1), weights, preferred_element_type=jnp.float32
        )
        o_ref[at, :] = total.astype(jnp.bfloat16)
        return carry

    lax.fori_loop(0, x_ref.shape[0] // block, body, 0)


def forward(rows, count, x, w):
    panels, slots, tile, _ = w.shape
    tokens, width = x.shape
    return pl.pallas_call(
        forward_kernel,
        grid_spec=pltpu.PrefetchScalarGridSpec(
            num_scalar_prefetch=2,
            grid=(panels,),
            in_specs=[
                pl.BlockSpec((tokens, width), lambda p, *_: (0, 0)),
                pl.BlockSpec((1, slots, tile, tile), lambda p, *_: (p, 0, 0, 0)),
            ],
            out_specs=pl.BlockSpec((tokens, tile), lambda p, *_: (0, p)),
        ),
        out_shape=jax.ShapeDtypeStruct((tokens, panels * tile), jnp.bfloat16),
        compiler_params=pltpu.CompilerParams(vmem_limit_bytes=VMEM_LIMIT),
        cost_estimate=pl.CostEstimate(
            flops=2 * tokens * panels * slots * tile * tile,
            bytes_accessed=2 * (tokens * width + w.size + tokens * panels * tile),
            transcendentals=0,
        ),
        name="forward",
    )(rows, count, x, w)


def transpose_kernel(x_ref, o_ref):
    o_ref[...] = x_ref[...].T


def transposed(x):
    tokens, width = x.shape
    step = 256
    return pl.pallas_call(
        transpose_kernel,
        grid=(width // step,),
        in_specs=[pl.BlockSpec((tokens, step), lambda i: (0, i))],
        out_specs=pl.BlockSpec((step, tokens), lambda i: (i, 0)),
        out_shape=jax.ShapeDtypeStruct((width, tokens), jnp.bfloat16),
        compiler_params=pltpu.CompilerParams(vmem_limit_bytes=16 * 1024 * 1024),
        cost_estimate=pl.CostEstimate(
            flops=0, bytes_accessed=4 * x.size, transcendentals=0
        ),
        name="transposed",
    )(x)


def weight_kernel(rows, count, xt_ref, g_ref, o_ref):
    panel = pl.program_id(0)
    slots, tile, _ = o_ref.shape[1:]
    live = count[panel]
    half = slots // 2
    for part in range(2):
        first = part * half

        @pl.when(live > first)
        def _():
            chosen = [xt_ref[rows[panel * slots + first + k]] for k in range(half)]
            total = jnp.dot(
                jnp.concatenate(chosen, axis=0), g_ref[...], preferred_element_type=jnp.float32
            )
            for k in range(half):
                block = total[k * tile : (k + 1) * tile]
                o_ref[0, first + k] = jnp.where(live > first + k, block, 0.0).astype(jnp.bfloat16)

        @pl.when(live <= first)
        def _():
            o_ref[0, first : first + half] = jnp.zeros((half, tile, tile), jnp.bfloat16)


def weight_grad(rows, count, xt, g, slots, tile):
    blocks, _, tokens = xt.shape
    panels = g.shape[1] // tile
    return pl.pallas_call(
        weight_kernel,
        grid_spec=pltpu.PrefetchScalarGridSpec(
            num_scalar_prefetch=2,
            grid=(panels,),
            in_specs=[
                pl.BlockSpec((blocks, tile, tokens), lambda p, *_: (0, 0, 0)),
                pl.BlockSpec((tokens, tile), lambda p, *_: (0, p)),
            ],
            out_specs=pl.BlockSpec((1, slots, tile, tile), lambda p, *_: (p, 0, 0, 0)),
        ),
        out_shape=jax.ShapeDtypeStruct((panels, slots, tile, tile), jnp.bfloat16),
        compiler_params=pltpu.CompilerParams(vmem_limit_bytes=VMEM_LIMIT),
        cost_estimate=pl.CostEstimate(
            flops=2 * tokens * panels * slots * tile * tile,
            bytes_accessed=2 * (xt.size + g.size + panels * slots * tile * tile),
            transcendentals=0,
        ),
        name="weight_grad",
    )(rows, count, xt, g)


def input_kernel(rows, count, g_ref, w_ref, o_ref, hits, found, total):
    row = pl.program_id(0)
    panels, slots, tile, _ = w_ref.shape
    blocks = pl.num_programs(0)

    @pl.when(row == 0)
    def _():
        def clear(r, carry):
            found[r] = 0
            return carry

        lax.fori_loop(0, blocks, clear, 0)

        def place(p, carry):
            for k in range(slots):

                @pl.when(count[p] > k)
                def _():
                    r = rows[p * slots + k]
                    n = found[r]
                    hits[r * panels + n] = p * slots + k
                    found[r] = n + 1

            return carry

        lax.fori_loop(0, panels, place, 0)

    n = found[row]
    total[...] = jnp.zeros_like(total)

    def pair(i, carry):
        first = hits[row * panels + 2 * i]
        both = 2 * i + 1 < n
        second = jnp.where(both, hits[row * panels + jnp.minimum(2 * i + 1, panels - 1)], first)
        p0, k0 = lax.div(first, slots), lax.rem(first, slots)
        p1, k1 = lax.div(second, slots), lax.rem(second, slots)
        weights = jnp.concatenate([w_ref[p0, k0], w_ref[p1, k1] * both.astype(jnp.bfloat16)], axis=1)
        grads = jnp.concatenate([g_ref[:, lanes(p0, tile)], g_ref[:, lanes(p1, tile)]], axis=1)
        total[...] += lax.dot_general(
            grads, weights, (((1,), (1,)), ((), ())), preferred_element_type=jnp.float32
        )
        return carry

    lax.fori_loop(0, lax.div(n + 1, 2), pair, 0)
    o_ref[...] = total[...].astype(jnp.bfloat16)


def input_grad(rows, count, g, w, blocks):
    panels, slots, tile, _ = w.shape
    tokens = g.shape[0]
    return pl.pallas_call(
        input_kernel,
        grid_spec=pltpu.PrefetchScalarGridSpec(
            num_scalar_prefetch=2,
            grid=(blocks,),
            in_specs=[
                pl.BlockSpec(g.shape, lambda r, *_: (0, 0)),
                pl.BlockSpec(w.shape, lambda r, *_: (0, 0, 0, 0)),
            ],
            out_specs=pl.BlockSpec((tokens, tile), lambda r, *_: (0, r)),
            scratch_shapes=[
                pltpu.SMEM((blocks * panels,), jnp.int32),
                pltpu.SMEM((blocks,), jnp.int32),
                pltpu.VMEM((tokens, tile), jnp.float32),
            ],
        ),
        out_shape=jax.ShapeDtypeStruct((tokens, blocks * tile), jnp.bfloat16),
        compiler_params=pltpu.CompilerParams(vmem_limit_bytes=VMEM_LIMIT),
        cost_estimate=pl.CostEstimate(
            flops=2 * tokens * panels * slots * tile * tile,
            bytes_accessed=2 * (g.size + w.size + tokens * blocks * tile),
            transcendentals=0,
        ),
        name="input_grad",
    )(rows, count, g, w)


def local(tokens, w_tiles, tile_rows, tile_count, grad_hidden):
    panels, slots, tile = w_tiles.shape[1:4]
    width = tokens.shape[1]
    blocks = width // tile
    rows, count, w = tile_rows.reshape(-1), tile_count.reshape(-1), w_tiles[0]

    gathered = lax.all_gather(tokens, "col", axis=0, tiled=True)
    partial_act = forward(rows, count, gathered, w)
    xt = transposed(gathered).reshape(blocks, tile, gathered.shape[0])
    pre_act = lax.psum_scatter(partial_act, "row", scatter_dimension=0, tiled=True)
    pre_act = pre_act.astype(jnp.float32)
    gelu_fn = partial(jax.nn.gelu, approximate=True)
    hidden, backward = jax.vjp(gelu_fn, pre_act)
    grad_pre = backward(grad_hidden.astype(jnp.float32))[0].astype(jnp.bfloat16)
    grad_all = lax.all_gather(grad_pre, "row", axis=0, tiled=True)

    grad_w = weight_grad(rows, count, xt, grad_all, slots, tile)
    grad_w = lax.psum(grad_w, "dp")
    grad_x = input_grad(rows, count, grad_all, w, blocks)
    grad_x = lax.psum_scatter(grad_x, "col", scatter_dimension=0, tiled=True)
    return hidden.astype(jnp.bfloat16), grad_x, grad_w[None]


def solution(mesh):
    return jax.shard_map(
        local,
        mesh=mesh,
        in_specs=(
            P(("dp", "col"), "row"),
            P("row", "col", None, None, None),
            P("row", "col", None),
            P("row", "col"),
            P(("dp", "row"), "col"),
        ),
        out_specs=(
            P(("dp", "row"), "col"),
            P(("dp", "col"), "row"),
            P("row", "col", None, None, None),
        ),
        check_vma=False,
    )
```

time: 724 us -> 434 us (0.60)
  local copies, waits for them, and re-layouts: 183 us -> 12.7 us
  other arithmetic: 141 us -> 3.52 us
  matrix products: 96.8 us -> 0 us
  waiting for transfers between devices: 284 us -> 348 us
  Pallas kernels: 0 us -> 55.2 us
    scatter-add x8 -> x0, other arithmetic: 104 us -> none  [input_per_block(): placed = placed.at[:, flat_rows, :].add(spread)]
    dot_general x16 -> x0, matrix products: 96.8 us -> none  [the longest x8 37.1 us: input_per_block(): jnp.einsum('tpc,pkbc->tpkb', row_block, masked, preferred_element_type=jn...]
    gather x12 -> x0, local copies, waits for them, and re-layouts: 83.2 us -> none  [select(): return jnp.take(shaped, slot_rows, axis=1)]
    psum x1, waiting for transfers between devices: 0.02 us -> 61.3 us  [local(): grad_w = lax.psum(grad_w, 'dp')]
    pallas_call x0 -> x4, Pallas kernels: none -> 55.2 us  [the longest x1 19.5 us: forward(): pl.pallas_call(forward_kernel, grid_spec=pltpu.PrefetchScalarGridSpec(num...]
    convert_element_type x10 -> x0, local copies, waits for them, and re-layouts: 33.1 us -> none  [the longest x8 19.8 us: settle(): values.astype(jnp.bfloat16)]
    while x36 -> x0, local copies, waits for them, and re-layouts: 24.3 us -> none  [the longest x3 12.7 us: local(): lax.map(hidden_per_block, blocks_in).reshape(row_count, panels * tile_size)]
    reshape x10 -> x1, local copies, waits for them, and re-layouts: 17.8 us -> 0.08 us  [local(): rows, count, w = (tile_rows.reshape(-1), tile_count.reshape(-1), w_tiles[0])]
  transfers between devices with their start and end apart: 5 -> 5, of which waited for: 4 -> 5; matrix products, arithmetic and copies ran while one was open for 28% -> 0% of each run, Pallas kernels for 0% -> 5%
where the time goes in v1:
time: 434 us; the launch traced here: 433 us
  waiting for transfers between devices  348 us (80%)
  Pallas kernels  55.2 us (13%)
  between operations  13.8 us (3%)
  local copies, waits for them, and re-layouts  12.7 us (3%)
    reduce_scatter x1, waiting for transfers between devices, local(): grad_x = lax.psum_scatter(grad_x, 'col', scatter_dimension=0, tiled=True)  114 us
    all_gather x1, waiting for transfers between devices, local(): gathered = lax.all_gather(tokens, 'col', axis=0, tiled=True)  102 us
    psum x1, waiting for transfers between devices, local(): grad_w = lax.psum(grad_w, 'dp')  61.3 us
    reduce_scatter x1, waiting for transfers between devices, local(): lax.psum_scatter(partial_act, 'row', scatter_dimension=0, tiled=True)  37.9 us
    all_gather x1, waiting for transfers between devices, local(): grad_all = lax.all_gather(grad_pre, 'row', axis=0, tiled=True)  31.9 us
    pallas_call x1, Pallas kernels, forward(): pl.pallas_call(forward_kernel, grid_spec=pltpu.PrefetchScalarGridSpec(num...  19.5 us
    pallas_call x1, Pallas kernels, input_grad(): pl.pallas_call(input_kernel, grid_spec=pltpu.PrefetchScalarGridSpec(num_s...  18.4 us
    pallas_call x1, Pallas kernels, weight_grad(): pl.pallas_call(weight_kernel, grid_spec=pltpu.PrefetchScalarGridSpec(num_...  14.1 us
  transfers between devices with their start and end apart: 5, of which 5 were waited for; matrix products, arithmetic and copies ran while one was open for 0% of the time, Pallas kernels for 5%

profile of v1, /device:TPU:8, one launch (start us, length us, event | category | flops | bytes accessed | tf_op | source)
XLA Modules:
  0.0 432.9 jit_solution(3357801473193291351)
XLA Ops:
  7.2 0.0 all-gather.3.cloned.1.call-start
  7.2 0.7 all-gather.3.cloned.1.call-update
  7.9 0.0 reduce-scatter.3.cloned.1.call-start
  7.9 0.8 copy.9
  8.7 0.1 reshape.15.rows
  8.8 101.7 %all-gather.3.cloned.1.call-done.x_ref = bf16[1024,3072]{1,0:T(8,128)(2,1)} async-done(((bf16[64,3072]{1,0:T(8,128)(2,1)}), bf16[1024,3072]{1,0:T(8,128)(2,1)}) %all-gather.3.cloned.1.call-update) | async-done | bytes 6291472 | tf_op jit(solution)/shard_map/all_gather | solution.py:215
  110.5 0.0 copy-start.3
  110.5 0.7 copy-done.3
  111.2 19.5 %forward.1 = bf16[1024,1536]{1,0:T(8,128)(2,1)} custom-call(s32[96]{0:T(128)S(1)} %reshape.15.rows, s32[12]{0:T(128)S(1)} %bitcast.5, bf16[1024,3072]{1,0:T(8,128)(2,1)} %all-gather.3.cloned.1.call-done.x_ref, bf16[12,8,128,128]{3,2,1,0:T(8,128)(2,1)} %bitcast.8), custom_call_target="tpu_custom_call" | custom-call | flops 3221225472 | bytes 12582912 | tf_op jit(solution)/shard_map/forward/pallas_call | solution.py:41
  130.7 0.0 reduce-scatter.3.cloned.1.call-update
  130.7 0.0 all-gather.5.cloned.1.call-start
  130.7 37.9 %reduce-scatter.3.cloned.1.call-done = bf16[256,1536]{1,0:T(8,128)(2,1)} async-done(((bf16[1024,1536]{1,0:T(8,128)(2,1)}), bf16[256,1536]{1,0:T(8,128)(2,1)}) %reduce-scatter.3.cloned.1.call-update) | async-done | bytes 786448 | tf_op jit(solution)/shard_map/reduce_scatter | solution.py:218
  168.7 0.0 copy-done.5
  168.7 3.5 fusion.3
  172.2 0.0 all-gather.5.cloned.1.call-update
  172.2 0.0 all-reduce.2.cloned.1.call-start
  172.3 0.0 copy-start
  172.3 2.8 copy-done
  175.1 3.3 transposed.1
  178.3 0.0 copy-start.1
  178.3 2.6 copy-done.1
  181.0 31.9 %all-gather.5.cloned.1.call-done.g_ref = bf16[1024,1536]{1,0:T(8,128)(2,1)} async-done(((bf16[256,1536]{1,0:T(8,128)(2,1)}), bf16[1024,1536]{1,0:T(8,128)(2,1)}) %all-gather.5.cloned.1.call-update) | async-done | bytes 3145744 | tf_op jit(solution)/shard_map/all_gather | solution.py:223
  212.8 0.0 copy-done.4
  212.8 14.1 %weight_grad.1 = bf16[12,8,128,128]{3,2,1,0:T(8,128)(2,1)} custom-call(s32[96]{0:T(128)S(1)} %reshape.15.rows, s32[12]{0:T(128)S(1)} %bitcast.6, bf16[24,128,1024]{2,1,0:T(8,128)(2,1)} %bitcast.4, bf16[1024,1536]{1,0:T(8,128)(2,1)} %all-gather.5.cloned.1.call-done.g_ref), custom_call_target="tpu_custom_call" | custom-call | flops 3221225472 | bytes 12582912 | tf_op jit(solution)/shard_map/weight_grad/pallas_call | solution.py:110
  226.9 0.0 all-reduce.2.cloned.1.call-update
  226.9 0.0 reduce-scatter.5.cloned.1.call-start
  227.0 1.8 copy-done.2
  228.8 18.4 %input_grad.1 = bf16[1024,3072]{1,0:T(8,128)(2,1)} custom-call(s32[96]{0:T(128)S(1)} %reshape.15.rows, s32[12]{0:T(128)S(1)} %bitcast.7, bf16[1024,1536]{1,0:T(8,128)(2,1)S(1)} %copy-done.2, bf16[12,8,128,128]{3,2,1,0:T(8,128)(2,1)} %bitcast.9), custom_call_target="tpu_custom_call" | custom-call | flops 3221225472 | bytes 12582912 | tf_op jit(solution)/shard_map/input_grad/pallas_call | solution.py:182
  247.2 0.0 reduce-scatter.5.cloned.1.call-update
  247.2 61.3 %all-reduce.2.cloned.1.call-done = bf16[1,12,8,128,128]{4,3,2,1,0:T(8,128)(2,1)} async-done(((bf16[1,12,8,128,128]{4,3,2,1,0:T(8,128)(2,1)}), bf16[1,12,8,128,128]{4,3,2,1,0:T(8,128)(2,1)}) %all-reduce.2.cloned.1.call-update) | async-done | bytes 3145744 | tf_op jit(solution)/shard_map/psum | solution.py:226
  308.5 113.9 %reduce-scatter.5.cloned.1.call-done = bf16[64,3072]{1,0:T(8,128)(2,1)} async-done(((bf16[1024,3072]{1,0:T(8,128)(2,1)}), bf16[64,3072]{1,0:T(8,128)(2,1)}) %reduce-scatter.5.cloned.1.call-update) | async-done | bytes 393232 | tf_op jit(solution)/shard_map/reduce_scatter | solution.py:228
  422.4 4.0 copy.11
  (3 shorter events, 0.0 us)
Async XLA Ops:
  7.2 103.4 %all-gather.3.cloned.1.call-start = ((), (), s32[]{:S(2)}) async-start(), calls=%async_computation.2 | async-start | bytes 6684672 | tf_op jit(solution)/shard_map/all_gather | solution.py:215
  7.9 160.8 %reduce-scatter.3.cloned.1.call-start = ((), (), s32[]{:S(2)}) async-start(), calls=%async_computation.3 | async-start | bytes 3932160 | tf_op jit(solution)/shard_map/reduce_scatter | solution.py:218
  110.5 0.7 copy-start.3
  130.7 38.0 %copy-start.5 = (bf16[256,1536]{1,0:T(8,128)(2,1)S(1)}, bf16[256,1536]{1,0:T(8,128)(2,1)}, u32[]{:S(2)}) copy-start(bf16[256,1536]{1,0:T(8,128)(2,1)} %param.9) | copy-start | bytes 2359300
  130.7 82.1 %all-gather.5.cloned.1.call-start = ((), (), s32[]{:S(2)}) async-start(), calls=%async_computation.4 | async-start | bytes 3932160 | tf_op jit(solution)/shard_map/all_gather | solution.py:223
  172.2 136.3 %all-reduce.2.cloned.1.call-start = ((), (), s32[]{:S(2)}) async-start(), calls=%async_computation.6 | async-start | bytes 6291456 | tf_op jit(solution)/shard_map/psum | solution.py:226
  172.3 2.8 copy-start
  175.1 37.8 %copy-start.4 = (s32[1,12]{1,0:T(1,128)S(1)}, s32[1,12]{1,0:T(1,128)}, u32[]{:S(2)}) copy-start(s32[1,12]{1,0:T(1,128)} %param.8) | copy-start | bytes 148
  178.3 2.6 copy-start.1
  226.9 1.9 copy-start.2
  226.9 195.5 %reduce-scatter.5.cloned.1.call-start = ((), (), s32[]{:S(2)}) async-start(), calls=%async_computation.5 | async-start | bytes 6684672 | tf_op jit(solution)/shard_map/reduce_scatter | solution.py:228
Sparse Core Ops, SparseCore 0:
  10.5 100.0 all-gather.2
  130.8 37.8 reduce-scatter.2
  172.3 40.4 all-gather.4
  227.1 81.4 all-reduce.1
  312.7 109.6 reduce-scatter.4
